TPU v7x, 128 devices: a whole 4x4x4 slice. The times are simulated.
128 devices in a mesh: dp: 8 (over x, core), seq: 16 (over z, y).
Axes of the slice: x: 4, y: 4, z: 4, core: 2. Of those that a mesh axis runs over, the one named last changes fastest.
Arguments:
- trunk: bfloat16 [8, 4096, 1536], P('dp', 'seq'), may hold values from -34 to 34
- skip: bfloat16 [8, 8192, 1536], P('dp', 'seq'), may hold values from -6 to 6
- valid_bins: int32 [8], P('dp'), may hold values from 2048 to 4096, as said below
- query_weight: bfloat16 [1536, 256], replicated
- key_weight: bfloat16 [1536, 256], replicated
- value_weight: bfloat16 [1536, 768], replicated, may hold values from -0.15625 to 0.15625
- out_weight: bfloat16 [768, 1536], replicated, may hold values from -0.21875 to 0.21875
- depth_weight: float32 [3, 1536], replicated, may hold values from -3 to 3
- point_weight: bfloat16 [1536, 1536], replicated, may hold values from -0.15625 to 0.15625
- cotangent: bfloat16 [8, 8192, 1536], P('dp', 'seq'), may hold values from -6 to 6
Outputs:
- grad_pointwise: bfloat16 [1536, 1536], replicated
- grad_depthwise: float32 [3, 1536], replicated
- grad_skip: bfloat16 [8, 8192, 1536], P('dp', 'seq')
Inputs may be any that keep to these rules, and one draw needn't show every extreme that they name: Bins at or past a window's valid_bins are padding; in every draw some window is whole.
All inputs are finite; a program needn't handle non-finite values.
Results may differ from a plain program's by a relative error of at most 0.017.
Values may be sent and summed in bfloat16 or wider, within the bound.
No kernel may reach another device: no remote copies, remote signals or barrier semaphores. Data moves between devices by JAX's collectives and lax.ppermute only.
A program may use at most 128 MiB of HBM per device.

v0:
```python
from functools import partial
import math
import jax
import jax.numpy as jnp
from jax import lax
from jax.sharding import PartitionSpec as P

H = 4
DH = 64
DV = 192


def padded_2(cells, sides, width):
    for axis, dim in sides:
        count = lax.axis_size(axis)
        ends = count - 1
        head = lax.slice_in_dim(cells, 0, width, axis=dim)
        tail = lax.slice_in_dim(cells, cells.shape[dim] - width, cells.shape[dim], axis=dim)
        cells = jnp.concatenate(
            [
                lax.ppermute(tail, axis, [(i, (i + 1) % count) for i in range(ends)]),
                cells,
                lax.ppermute(head, axis, [((i + 1) % count, i) for i in range(ends)]),
            ],
            axis=dim,
        )
    return cells


def local(
    trunk,
    skip,
    valid_bins,
    query_weight,
    key_weight,
    value_weight,
    out_weight,
    depth_weight,
    point_weight,
    cotangent,
):
    tokens = trunk[0]
    row_count = tokens.shape[0]
    score_scale = 1.0 / math.sqrt(DH)
    queries = (
        jnp.dot(tokens, query_weight, preferred_element_type=jnp.float32)
        .astype(jnp.bfloat16)
        .reshape(row_count, H, DH)
    )
    keys = jnp.dot(tokens, key_weight, preferred_element_type=jnp.float32).astype(jnp.bfloat16)
    values = jnp.dot(tokens, value_weight, preferred_element_type=jnp.float32).astype(jnp.bfloat16)
    limit = valid_bins[0]
    running_max = jnp.full((H, row_count), -1e30, jnp.float32)
    weighted = jnp.zeros((row_count, H, DV), jnp.float32)
    key_piece = lax.all_gather(keys, "seq", axis=0, tiled=True)
    value_piece = lax.all_gather(values, "seq", axis=0, tiled=True)
    width = key_piece.shape[0]
    key_heads = key_piece.reshape(width, H, DH)
    value_heads = value_piece.reshape(width, H, DV)
    scores = (
        jnp.einsum("qhd,khd->hqk", queries, key_heads, preferred_element_type=jnp.float32)
        * score_scale
    )
    places = jnp.arange(width, dtype=jnp.int32)
    scores = jnp.where(places[None, None, :] < limit, scores, -1e30)
    fresh_max = jnp.maximum(running_max, jnp.max(scores, axis=2))
    shrink = jnp.exp(running_max - fresh_max)
    weights_raw = jnp.exp(scores - fresh_max[:, :, None])
    running_total = jnp.sum(weights_raw, axis=2)
    update = jnp.einsum(
        "hqk,khd->qhd",
        weights_raw.astype(jnp.bfloat16),
        value_heads,
        preferred_element_type=jnp.float32,
    )
    weighted = weighted * shrink.T[:, :, None] + update
    running_max, running_total, weighted = (fresh_max, running_total, weighted)
    mixed = (weighted / running_total.T[:, :, None]).reshape(row_count, H * DV)
    attended = (mixed * lax.rsqrt(jnp.mean(mixed * mixed, axis=1, keepdims=True) + 1e-05)).astype(
        jnp.bfloat16
    )
    hidden = (
        tokens.astype(jnp.float32)
        + jnp.dot(attended, out_weight, preferred_element_type=jnp.float32)
    ).astype(jnp.bfloat16)
    upsampled = (
        jnp.repeat(hidden, 2, axis=0).astype(jnp.float32) + skip[0].astype(jnp.float32)
    ).astype(jnp.bfloat16)
    padded = padded_2(upsampled, (("seq", 0),), 1)
    pre_act = (
        depth_weight[0] * padded[:-2]
        + depth_weight[1] * padded[1:-1]
        + depth_weight[2] * padded[2:]
    )
    act_value, pullback = jax.vjp(partial(jax.nn.gelu, approximate=True), pre_act)
    activated = act_value.astype(jnp.bfloat16)
    upstream = cotangent[0]
    grad_act = lax.dot_general(
        upstream, point_weight, (((1,), (1,)), ((), ())), preferred_element_type=jnp.float32
    )
    grad_pre = pullback(grad_act)[0].astype(jnp.bfloat16)
    fine_rows = grad_pre.shape[0]
    grad_wide = grad_pre.astype(jnp.float32)
    depth_term = jnp.stack(
        [
            jnp.sum(padded[offset : offset + fine_rows].astype(jnp.float32) * grad_wide, axis=0)
            for offset in range(3)
        ]
    )
    grad_padded = padded_2(grad_pre, (("seq", 0),), 1)
    grad_skip = (
        depth_weight[0] * grad_padded[2:]
        + depth_weight[1] * grad_padded[1:-1]
        + depth_weight[2] * grad_padded[:-2]
    ).astype(jnp.bfloat16)
    norm_scale = 1.0 / math.sqrt(lax.axis_size("dp") * lax.axis_size("seq") * fine_rows)
    point_term = lax.dot_general(
        activated, upstream, (((0,), (0,)), ((), ())), preferred_element_type=jnp.float32
    )
    point_total, depth_total = lax.psum((point_term, depth_term), ("dp", "seq"))
    grad_pointwise = (point_total * norm_scale).astype(jnp.bfloat16)
    return (grad_pointwise, depth_total * norm_scale, grad_skip[None])


def solution(mesh):
    return jax.shard_map(
        local,
        mesh=mesh,
        in_specs=(
            P("dp", "seq", None),
            P("dp", "seq", None),
            P("dp"),
            P(),
            P(),
            P(),
            P(),
            P(),
            P(),
            P("dp", "seq", None),
        ),
        out_specs=(P(), P(), P("dp", "seq", None)),
        check_vma=False,
    )
```

profile of v0, /device:TPU:1, one launch (start us, length us, event | category | flops | bytes accessed | tf_op | source)
XLA Modules:
  0.0 349.5 jit_solution(12524377417579679030)
XLA Ops:
  7.2 0.0 copy-start
  7.2 0.0 copy-start.3
  7.2 0.0 all-gather.3.cloned.1.call-start
  7.2 2.6 convolution_convert_fusion.1
  9.8 0.0 all-gather.3.cloned.1.call-update
  9.8 0.0 all-gather.5.cloned.1.call-start
  9.9 3.4 convolution_convert_fusion
  13.3 0.0 all-gather.5.cloned.1.call-update
  13.4 0.0 all-reduce.2.cloned.1.call-start
  14.1 0.0 copy-done.3
  14.1 1.6 convolution_convert_fusion.2
  15.7 42.6 %all-gather.3.cloned.1.call-done = bf16[4096,256]{1,0:T(8,128)(2,1)} async-done(((bf16[256,256]{1,0:T(8,128)(2,1)}), bf16[4096,256]{1,0:T(8,128)(2,1)}) %all-gather.3.cloned.1.call-update) | async-done | bytes 2097168 | tf_op jit(solution)/shard_map/all_gather | solution.py:55
  58.2 4.1 %copy.15 = bf16[4096,256]{0,1:T(8,128)(2,1)} copy(bf16[4096,256]{1,0:T(8,128)(2,1)} %all-gather.3.cloned.1.call-done) | data formatting | bytes 4194304 | tf_op jit(solution)/shard_map/all_gather | solution.py:55
  62.3 4.1 %fusion = (f32[4,256]{1,0:T(4,128)S(1)}, f32[4,256,4096]{2,1,0:T(8,128)S(1)}) fusion(pred[4096]{0:T(1024)(128)(4,1)S(1)} %iota_compare_fusion, bf16[256,4,64]{0,2,1:T(8,128)(2,1)S(1)} %bitcast.49, bf16[4096,4,64]{0,2,1:T(8,128)(2,1)} %bitcast.47), kind=kOutput, calls=%fused_computation.2 | convolution fusion | flops 549452800 | bytes 19013632 | tf_op jit(solution)/shard_map/qhd,khd->hqk/dot_general | solution.py:61
  66.4 0.0 copy-start.2
  66.4 5.9 %copy-done.2 = f32[4,256,4096]{2,1,0:T(8,128)} copy-done((f32[4,256,4096]{2,1,0:T(8,128)}, f32[4,256,4096]{2,1,0:T(8,128)S(1)}, u32[]{:S(2)}) %copy-start.2) | copy-done | bytes 16777240
  72.4 4.0 %fusion.1 = f32[4,256]{1,0:T(4,128)S(1)} fusion(f32[4,256,4096]{2,1,0:T(8,128)S(1)} %get-tuple-element.17, f32[4,256]{1,0:T(4,128)S(1)} %get-tuple-element.15, pred[4096]{0:T(1024)(128)(4,1)S(1)} %iota_compare_fusion), kind=kLoop, calls=%fused_computation.3 | loop fusion | flops 16776192 | bytes 16789504 | tf_op jit(solution)/shard_map/reduce_sum | solution.py:69
  76.4 46.3 %all-gather.5.cloned.1.call-done = bf16[4096,768]{1,0:T(8,128)(2,1)} async-done(((bf16[256,768]{1,0:T(8,128)(2,1)}), bf16[4096,768]{1,0:T(8,128)(2,1)}) %all-gather.5.cloned.1.call-update) | async-done | bytes 6291472 | tf_op jit(solution)/shard_map/all_gather | solution.py:56
  122.7 8.6 %copy.16 = bf16[4096,768]{0,1:T(8,128)(2,1)} copy(bf16[4096,768]{1,0:T(8,128)(2,1)} %all-gather.5.cloned.1.call-done) | data formatting | bytes 12582912 | tf_op jit(solution)/shard_map/all_gather | solution.py:56
  131.3 10.3 %multiply_reduce_fusion = (f32[256]{0:T(256)S(1)}, f32[256,4,192]{0,2,1:T(8,128)S(1)}) fusion(f32[256,4]{0,1:T(4,128)S(1)} %bitcast.50, bf16[4096,4,192]{0,2,1:T(8,128)(2,1)} %bitcast.48, f32[4,256,4096]{2,1,0:T(8,128)} %copy-done.2, f32[4,256]{1,0:T(4,128)S(1)} %get-tuple-element.15, pred[4096]{0:T(1024)(128)(4,1)S(1)} %iota_compare_fusion, ...), kind=kOutput, calls=%fused_computation.68 | convolution fusion | flops 1628176128 | bytes 23872512 | tf_op jit(solution)/shard_map/hqk,khd->qhd/dot_general | solution.py:70
  141.6 0.1 fusion.51
  141.7 0.0 copy-done
  141.7 0.8 fusion.26
  142.5 2.7 broadcast_in_dim.33
  145.2 5.2 %convert_element_type.79 = f32[512,1536]{1,0:T(8,128)} reshape(f32[256,2,1536]{2,1,0:T(2,128)} %broadcast_in_dim.33) | data formatting | bytes 6291456 | tf_op jit(solution)/shard_map/convert_element_type | solution.py:87
  150.5 0.0 copy-start.4
  150.5 0.0 copy-start.5
  150.5 2.9 fusion.24
  153.4 3.1 collective-permute-start
  156.6 1.5 collective-permute-start.1
  158.0 0.0 copy-done.4
  158.0 0.1 slice_reduce_fusion.2
  158.1 0.0 collective-permute-done
  158.1 2.8 collective-permute-done.1
  160.9 0.0 copy-done.5
  160.9 6.6 %fusion.27 = f32[1536,1536]{1,0:T(8,128)} fusion(bf16[512,1536]{1,0:T(8,128)(2,1)S(1)} %fusion.24, bf16[1,1536]{1,0:T(2,128)(2,1)S(1)} %collective-permute-done.1, bf16[1,1536]{1,0:T(2,128)(2,1)S(1)} %collective-permute-done, bf16[1,512,1536]{2,1,0:T(8,128)(2,1)S(1)} %copy-done.5, f32[1536]{0:T(1024)S(1)} %get-tuple-element.7, ...), kind=kOutput, calls=%fused_computation.41 | convolution fusion | flops 2434007040 | bytes 12607488 | tf_op jit(solution)/shard_map/dot_general | solution.py:117
  167.5 0.0 all-reduce.2.cloned.1.call-update
  167.5 7.5 %fusion.17 = bf16[512,1536]{1,0:T(8,128)(2,1)S(1)} fusion(bf16[1,1536]{1,0:T(2,128)(2,1)S(1)} %collective-permute-done.1, bf16[512,1536]{1,0:T(8,128)(2,1)S(1)} %fusion.24, bf16[1,1536]{1,0:T(2,128)(2,1)S(1)} %collective-permute-done, bf16[1536,1536]{1,0:T(8,128)(2,1)} %param.18, bf16[1,512,1536]{2,1,0:T(8,128)(2,1)} %param.19, ...), kind=kOutput, calls=%fused_computation.28 | convolution fusion | flops 2442657792 | bytes 9461760 | tf_op jit(solution)/shard_map/dot_general | solution.py:98
  175.1 1.3 collective-permute-start.2
  176.4 4.0 %collective-permute-start.3 = (bf16[1,1536]{1,0:T(2,128)(2,1)S(1)}, bf16[1,1536]{1,0:T(2,128)(2,1)S(1)}, u32[]{:S(2)}, u32[]{:S(2)}) collective-permute-start(bf16[1,1536]{1,0:T(2,128)(2,1)S(1)} %get-tuple-element.11), channel_id=1, source_target_pairs={{0,1},{1,2},{2,3},{3,4},{4,5},{5,6},{6,7},{7,8},{8,9},{9,10},{10,1... | collective-permute-start | bytes 9224 | tf_op jit(solution)/shard_map/ppermute | solution.py:21
  180.4 0.0 collective-permute-done.2
  180.4 0.7 collective-permute-done.3
  181.1 3.5 %fusion.18 = (f32[1536]{0:T(1024)S(1)}, f32[1536]{0:T(1024)S(1)}, f32[1536]{0:T(1024)S(1)}, bf16[1,512,1536]{2,1,0:T(8,128)(2,1)}) fusion(bf16[512,1536]{1,0:T(8,128)(2,1)S(1)} %fusion.17, bf16[512,1536]{1,0:T(8,128)(2,1)S(1)} %fusion.24, bf16[1,1536]{1,0:T(2,128)(2,1)S(1)} %collective-permute-done, bf16[1,1536]{1,0:T(2,128)(2,1)S(1)} %collective-permute-done.1, ...), kind=kLoop, calls=%fused_computation.29 | loop fusion | flops 23588352 | bytes 4767744 | tf_op jit(solution)/shard_map/reduce_sum | solution.py:106
  184.7 74.9 %psum.15 = f32[3,1536]{1,0:T(4,128)S(1)} all-reduce(f32[3,1536]{1,0:T(4,128)S(1)} %pad_maximum_fusion.5), channel_id=1, replica_groups=mesh['dp'=8,'seq'=16] {'dp','seq'}, use_global_device_ids=true, to_apply=%region_7.8 | all-reduce | flops 4608 | bytes 36864 | tf_op jit(solution)/shard_map/psum | solution.py:120
  259.6 0.6 broadcast_multiply_fusion
  260.2 75.5 %all-reduce.2.cloned.1.call-done = f32[1536,1536]{1,0:T(8,128)} async-done(((f32[1536,1536]{1,0:T(8,128)}), f32[1536,1536]{1,0:T(8,128)}) %all-reduce.2.cloned.1.call-update) | async-done | bytes 9437200 | tf_op jit(solution)/shard_map/psum | solution.py:120
  335.7 0.0 copy-start.1
  335.7 7.2 %multiply_convert_fusion = bf16[1536,1536]{1,0:T(8,128)(2,1)} fusion(f32[1536,1536]{1,0:T(8,128)} %all-reduce.2.cloned.1.call-done), kind=kLoop, calls=%fused_computation.5 | loop fusion | flops 4718592 | bytes 14155776 | tf_op jit(solution)/shard_map/convert_element_type | solution.py:121
  343.0 0.0 copy-done.1
  (9 shorter events, 0.1 us)
Async XLA Ops:
  7.2 134.5 %copy-start = (bf16[768,1536]{1,0:T(8,128)(2,1)S(1)}, bf16[768,1536]{1,0:T(8,128)(2,1)}, u32[]{:S(2)}) copy-start(bf16[768,1536]{1,0:T(8,128)(2,1)} %param.16) | copy-start | bytes 7077892
  7.2 6.9 %copy-start.3 = (bf16[1,256,1536]{2,1,0:T(8,128)(2,1)S(1)}, bf16[1,256,1536]{2,1,0:T(8,128)(2,1)}, u32[]{:S(2)}) copy-start(bf16[1,256,1536]{2,1,0:T(8,128)(2,1)} %param.10) | copy-start | bytes 2359300
  7.2 51.0 %all-gather.3.cloned.1.call-start = ((), (), s32[]{:S(2)}) async-start(), calls=%async_computation | async-start | bytes 2228224 | tf_op jit(solution)/shard_map/all_gather | solution.py:55
  9.8 112.8 %all-gather.5.cloned.1.call-start = ((), (), s32[]{:S(2)}) async-start(), calls=%async_computation.1 | async-start | bytes 6684672 | tf_op jit(solution)/shard_map/all_gather | solution.py:56
  13.4 322.4 %all-reduce.2.cloned.1.call-start = ((), (), s32[]{:S(2)}) async-start(), calls=%async_computation.2 | async-start | bytes 18874368 | tf_op jit(solution)/shard_map/psum | solution.py:120
  66.4 6.0 %copy-start.2 = (f32[4,256,4096]{2,1,0:T(8,128)}, f32[4,256,4096]{2,1,0:T(8,128)S(1)}, u32[]{:S(2)}) copy-start(f32[4,256,4096]{2,1,0:T(8,128)S(1)} %get-tuple-element.17) | copy-start | bytes 50331652
  150.5 7.6 %copy-start.4 = (f32[3,1536]{1,0:T(4,128)S(1)}, f32[3,1536]{1,0:T(4,128)}, u32[]{:S(2)}) copy-start(f32[3,1536]{1,0:T(4,128)} %param.17) | copy-start | bytes 55300
  150.5 10.4 %copy-start.5 = (bf16[1,512,1536]{2,1,0:T(8,128)(2,1)S(1)}, bf16[1,512,1536]{2,1,0:T(8,128)(2,1)}, u32[]{:S(2)}) copy-start(bf16[1,512,1536]{2,1,0:T(8,128)(2,1)} %param.19) | copy-start | bytes 4718596
  153.4 4.7 %collective-permute-start = (bf16[1,1536]{1,0:T(2,128)(2,1)S(1)}, bf16[1,1536]{1,0:T(2,128)(2,1)S(1)}, u32[]{:S(2)}, u32[]{:S(2)}) collective-permute-start(bf16[1,1536]{1,0:T(2,128)(2,1)S(1)} %get-tuple-element.12), channel_id=1, source_target_pairs={{0,1},{1,2},{2,3},{3,4},{4,5},{5,6},{6,7},{7,8},{8,9},{9,10},{10,1... | collective-permute-start | bytes 9224 | tf_op jit(solution)/shard_map/ppermute | solution.py:21
  156.6 4.4 %collective-permute-start.1 = (bf16[1,1536]{1,0:T(2,128)(2,1)S(1)}, bf16[1,1536]{1,0:T(2,128)(2,1)S(1)}, u32[]{:S(2)}, u32[]{:S(2)}) collective-permute-start(bf16[1,1536]{1,0:T(2,128)(2,1)S(1)} %get-tuple-element.13), channel_id=1, source_target_pairs={{1,0},{2,1},{3,2},{4,3},{5,4},{6,5},{7,6},{8,7},{9,8},{10,9},{11,1... | collective-permute-start | bytes 9224 | tf_op jit(solution)/shard_map/ppermute | solution.py:23
  175.1 5.3 %collective-permute-start.2 = (bf16[1,1536]{1,0:T(2,128)(2,1)S(1)}, bf16[1,1536]{1,0:T(2,128)(2,1)S(1)}, u32[]{:S(2)}, u32[]{:S(2)}) collective-permute-start(bf16[1,1536]{1,0:T(2,128)(2,1)S(1)} %get-tuple-element.10), channel_id=1, source_target_pairs={{1,0},{2,1},{3,2},{4,3},{5,4},{6,5},{7,6},{8,7},{9,8},{10,9},{11,1... | collective-permute-start | bytes 9224 | tf_op jit(solution)/shard_map/ppermute | solution.py:23
  176.4 4.8 %collective-permute-start.3 = (bf16[1,1536]{1,0:T(2,128)(2,1)S(1)}, bf16[1,1536]{1,0:T(2,128)(2,1)S(1)}, u32[]{:S(2)}, u32[]{:S(2)}) collective-permute-start(bf16[1,1536]{1,0:T(2,128)(2,1)S(1)} %get-tuple-element.11), channel_id=1, source_target_pairs={{0,1},{1,2},{2,3},{3,4},{4,5},{5,6},{6,7},{7,8},{8,9},{9,10},{10,1... | collective-permute-start | bytes 9224 | tf_op jit(solution)/shard_map/ppermute | solution.py:21
  335.7 7.2 %copy-start.1 = (bf16[768,1536]{1,0:T(8,128)(2,1)S(1)}, bf16[768,1536]{1,0:T(8,128)(2,1)}, u32[]{:S(2)}) copy-start(bf16[768,1536]{1,0:T(8,128)(2,1)} %param.16) | copy-start | bytes 7077892
Sparse Core Ops, SparseCore 0:
  10.7 47.4 all-gather.2
  60.9 61.6 all-gather.4
  167.6 168.0 all-reduce.1
where the time goes:
time: 350 us
  waiting for transfers between devices  168 us (48%)
  blocking collectives  74.9 us (21%)
  matrix products  36.9 us (11%)
  local copies, waits for them, and re-layouts  26.7 us (8%)
  other arithmetic  18.4 us (5%)
  between operations  14.6 us (4%)
  starting transfers between devices  9.98 us (3%)
    psum x1, waiting for transfers between devices, local(): point_total, depth_total = lax.psum((point_term, depth_term), ('dp', 'seq'))  75.5 us
    psum x1, blocking collectives, local(): point_total, depth_total = lax.psum((point_term, depth_term), ('dp', 'seq'))  74.9 us
    all_gather x1, waiting for transfers between devices, local(): value_piece = lax.all_gather(values, 'seq', axis=0, tiled=True)  46.3 us
    all_gather x1, waiting for transfers between devices, local(): key_piece = lax.all_gather(keys, 'seq', axis=0, tiled=True)  42.6 us
    dot_general x1, matrix products, local(): jnp.einsum('hqk,khd->qhd', weights_raw.astype(jnp.bfloat16), value_heads,...  10.3 us
    all_gather x1, local copies, waits for them, and re-layouts, local(): value_piece = lax.all_gather(values, 'seq', axis=0, tiled=True)  8.63 us
    dot_general x1, matrix products, local(): lax.dot_general(upstream, point_weight, (((1,), (1,)), ((), ())), preferr...  7.54 us
    convert_element_type x1, other arithmetic, local(): grad_pointwise = (point_total * norm_scale).astype(jnp.bfloat16)  7.24 us
  transfers between devices with their start and end apart: 7, of which 5 were waited for; matrix products, arithmetic and copies ran while one was open for 8% of the time, Pallas kernels for 0%

commit v1 on v0

--- a/solution.py
+++ b/solution.py
@@ -117,7 +117,7 @@
     point_term = lax.dot_general(
         activated, upstream, (((0,), (0,)), ((), ())), preferred_element_type=jnp.float32
     )
-    point_total, depth_total = lax.psum((point_term, depth_term), ("dp", "seq"))
+    point_total, depth_total = lax.psum(lax.psum((point_term, depth_term), "seq"), "dp")
     grad_pointwise = (point_total * norm_scale).astype(jnp.bfloat16)
     return (grad_pointwise, depth_total * norm_scale, grad_skip[None])
 

time: 350 us -> 452 us (1.29)
  waiting for transfers between devices: 168 us -> 248 us
  blocking collectives: 74.9 us -> 96 us
    psum x1 -> x2, waiting for transfers between devices: 75.5 us -> 156 us  [the longest x1 154 us: local(): lax.psum((point_term, depth_term), 'seq')]
    psum x1 -> x2, blocking collectives: 74.9 us -> 96 us  [the longest x1 59 us: local(): lax.psum((point_term, depth_term), 'seq')]
  transfers between devices with their start and end apart: 7 -> 8, of which waited for: 5 -> 6; matrix products, arithmetic and copies ran while one was open for 8% -> 6% of each run, Pallas kernels for 0% -> 0%
where the time goes in v1:
time: 452 us; the launch traced here: 451 us
  waiting for transfers between devices  248 us (55%)
  blocking collectives  96 us (21%)
  matrix products  36.9 us (8%)
  local copies, waits for them, and re-layouts  26.7 us (6%)
  other arithmetic  18.4 us (4%)
  between operations  14.6 us (3%)
  starting transfers between devices  10 us (2%)
    psum x1, waiting for transfers between devices, local(): lax.psum((point_term, depth_term), 'seq')  154 us
    psum x1, blocking collectives, local(): lax.psum((point_term, depth_term), 'seq')  59 us
    all_gather x1, waiting for transfers between devices, local(): value_piece = lax.all_gather(values, 'seq', axis=0, tiled=True)  46.3 us
    all_gather x1, waiting for transfers between devices, local(): key_piece = lax.all_gather(keys, 'seq', axis=0, tiled=True)  42.6 us
    psum x1, blocking collectives, local(): lax.psum(lax.psum((point_term, depth_term), 'seq'), 'dp')  37 us
    dot_general x1, matrix products, local(): jnp.einsum('hqk,khd->qhd', weights_raw.astype(jnp.bfloat16), value_heads,...  10.3 us
  transfers between devices with their start and end apart: 8, of which 6 were waited for; matrix products, arithmetic and copies ran while one was open for 6% of the time, Pallas kernels for 0%

profile of v1, /device:TPU:1, one launch (start us, length us, event | category | flops | bytes accessed | tf_op | source)
XLA Modules:
  0.0 451.0 jit_solution(2276133366466179838)
XLA Ops:
  7.2 0.0 copy-start
  7.2 0.0 copy-start.3
  7.2 0.0 all-gather.3.cloned.1.call-start
  7.2 2.6 convolution_convert_fusion.1
  9.8 0.0 all-gather.3.cloned.1.call-update
  9.8 0.0 all-gather.5.cloned.1.call-start
  9.9 3.4 convolution_convert_fusion
  13.3 0.0 all-gather.5.cloned.1.call-update
  13.4 0.0 all-reduce.3.cloned.1.call-start
  14.1 0.0 copy-done.3
  14.1 1.6 convolution_convert_fusion.2
  15.7 42.6 %all-gather.3.cloned.1.call-done = bf16[4096,256]{1,0:T(8,128)(2,1)} async-done(((bf16[256,256]{1,0:T(8,128)(2,1)}), bf16[4096,256]{1,0:T(8,128)(2,1)}) %all-gather.3.cloned.1.call-update) | async-done | bytes 2097168 | tf_op jit(solution)/shard_map/all_gather | solution.py:55
  58.2 4.1 copy.15
  62.3 4.1 fusion
  66.4 0.0 copy-start.2
  66.4 5.9 %copy-done.2 = f32[4,256,4096]{2,1,0:T(8,128)} copy-done((f32[4,256,4096]{2,1,0:T(8,128)}, f32[4,256,4096]{2,1,0:T(8,128)S(1)}, u32[]{:S(2)}) %copy-start.2) | copy-done | bytes 16777240
  72.4 4.0 fusion.1
  76.4 46.3 %all-gather.5.cloned.1.call-done = bf16[4096,768]{1,0:T(8,128)(2,1)} async-done(((bf16[256,768]{1,0:T(8,128)(2,1)}), bf16[4096,768]{1,0:T(8,128)(2,1)}) %all-gather.5.cloned.1.call-update) | async-done | bytes 6291472 | tf_op jit(solution)/shard_map/all_gather | solution.py:56
  122.7 8.6 %copy.16 = bf16[4096,768]{0,1:T(8,128)(2,1)} copy(bf16[4096,768]{1,0:T(8,128)(2,1)} %all-gather.5.cloned.1.call-done) | data formatting | bytes 12582912 | tf_op jit(solution)/shard_map/all_gather | solution.py:56
  131.3 10.3 %multiply_reduce_fusion = (f32[256]{0:T(256)S(1)}, f32[256,4,192]{0,2,1:T(8,128)S(1)}) fusion(f32[256,4]{0,1:T(4,128)S(1)} %bitcast.50, bf16[4096,4,192]{0,2,1:T(8,128)(2,1)} %bitcast.48, f32[4,256,4096]{2,1,0:T(8,128)} %copy-done.2, f32[4,256]{1,0:T(4,128)S(1)} %get-tuple-element.15, pred[4096]{0:T(1024)(128)(4,1)S(1)} %iota_compare_fusion, ...), kind=kOutput, calls=%fused_computation.68 | convolution fusion | flops 1628176128 | bytes 23872512 | tf_op jit(solution)/shard_map/hqk,khd->qhd/dot_general | solution.py:70
  141.6 0.1 fusion.51
  141.7 0.0 copy-done
  141.7 0.8 fusion.26
  142.5 2.7 broadcast_in_dim.33
  145.2 5.2 %convert_element_type.79 = f32[512,1536]{1,0:T(8,128)} reshape(f32[256,2,1536]{2,1,0:T(2,128)} %broadcast_in_dim.33) | data formatting | bytes 6291456 | tf_op jit(solution)/shard_map/convert_element_type | solution.py:87
  150.5 0.0 copy-start.4
  150.5 0.0 copy-start.5
  150.5 2.9 fusion.24
  153.4 3.1 collective-permute-start
  156.6 1.5 collective-permute-start.1
  158.0 0.0 copy-done.4
  158.0 0.1 slice_reduce_fusion.2
  158.1 0.0 collective-permute-done
  158.1 2.8 collective-permute-done.1
  160.9 0.0 copy-done.5
  160.9 6.6 %fusion.27 = f32[1536,1536]{1,0:T(8,128)} fusion(bf16[512,1536]{1,0:T(8,128)(2,1)S(1)} %fusion.24, bf16[1,1536]{1,0:T(2,128)(2,1)S(1)} %collective-permute-done.1, bf16[1,1536]{1,0:T(2,128)(2,1)S(1)} %collective-permute-done, bf16[1,512,1536]{2,1,0:T(8,128)(2,1)S(1)} %copy-done.5, f32[1536]{0:T(1024)S(1)} %get-tuple-element.7, ...), kind=kOutput, calls=%fused_computation.41 | convolution fusion | flops 2434007040 | bytes 12607488 | tf_op jit(solution)/shard_map/dot_general | solution.py:117
  167.5 0.0 all-reduce.3.cloned.1.call-update
  167.5 0.0 all-reduce.5.cloned.1.call-start
  167.6 154.1 %all-reduce.3.cloned.1.call-done = f32[1536,1536]{1,0:T(8,128)} async-done(((f32[1536,1536]{1,0:T(8,128)}), f32[1536,1536]{1,0:T(8,128)}) %all-reduce.3.cloned.1.call-update) | async-done | bytes 9437200 | tf_op jit(solution)/shard_map/psum | solution.py:120
  321.7 0.0 all-reduce.5.cloned.1.call-update
  321.7 7.5 %fusion.17 = bf16[512,1536]{1,0:T(8,128)(2,1)S(1)} fusion(bf16[1,1536]{1,0:T(2,128)(2,1)S(1)} %collective-permute-done.1, bf16[512,1536]{1,0:T(8,128)(2,1)S(1)} %fusion.24, bf16[1,1536]{1,0:T(2,128)(2,1)S(1)} %collective-permute-done, bf16[1536,1536]{1,0:T(8,128)(2,1)} %param.18, bf16[1,512,1536]{2,1,0:T(8,128)(2,1)} %param.19, ...), kind=kOutput, calls=%fused_computation.28 | convolution fusion | flops 2442657792 | bytes 9461760 | tf_op jit(solution)/shard_map/dot_general | solution.py:98
  329.3 1.3 collective-permute-start.2
  330.6 4.0 collective-permute-start.3
  334.6 0.0 collective-permute-done.2
  334.6 0.7 collective-permute-done.3
  335.3 3.5 fusion.18
  338.9 59.0 %psum.30 = f32[3,1536]{1,0:T(4,128)S(1)} all-reduce(f32[3,1536]{1,0:T(4,128)S(1)} %pad_maximum_fusion.5), channel_id=1, replica_groups=mesh['dp'=8,'seq'=16] {'seq'}, use_global_device_ids=true, to_apply=%region_8.9 | all-reduce | flops 4608 | bytes 36864 | tf_op jit(solution)/shard_map/psum | solution.py:120
  397.9 37.0 %psum.31 = f32[3,1536]{1,0:T(4,128)S(1)} all-reduce(f32[3,1536]{1,0:T(4,128)S(1)} %psum.30), channel_id=1, replica_groups=mesh['dp'=8,'seq'=16] {'dp'}, use_global_device_ids=true, to_apply=%region_9.10 | all-reduce | flops 4608 | bytes 36864 | tf_op jit(solution)/shard_map/psum | solution.py:120
  434.9 0.6 broadcast_multiply_fusion
  435.5 1.7 all-reduce.5.cloned.1.call-done
  437.2 0.0 copy-start.1
  437.2 7.2 %multiply_convert_fusion = bf16[1536,1536]{1,0:T(8,128)(2,1)} fusion(f32[1536,1536]{1,0:T(8,128)} %all-reduce.5.cloned.1.call-done), kind=kLoop, calls=%fused_computation.5 | loop fusion | flops 4718592 | bytes 14155776 | tf_op jit(solution)/shard_map/convert_element_type | solution.py:121
  444.5 0.0 copy-done.1
  (9 shorter events, 0.1 us)
Async XLA Ops:
  7.2 134.5 %copy-start = (bf16[768,1536]{1,0:T(8,128)(2,1)S(1)}, bf16[768,1536]{1,0:T(8,128)(2,1)}, u32[]{:S(2)}) copy-start(bf16[768,1536]{1,0:T(8,128)(2,1)} %param.16) | copy-start | bytes 7077892
  7.2 6.9 %copy-start.3 = (bf16[1,256,1536]{2,1,0:T(8,128)(2,1)S(1)}, bf16[1,256,1536]{2,1,0:T(8,128)(2,1)}, u32[]{:S(2)}) copy-start(bf16[1,256,1536]{2,1,0:T(8,128)(2,1)} %param.10) | copy-start | bytes 2359300
  7.2 51.0 %all-gather.3.cloned.1.call-start = ((), (), s32[]{:S(2)}) async-start(), calls=%async_computation | async-start | bytes 2228224 | tf_op jit(solution)/shard_map/all_gather | solution.py:55
  9.8 112.8 %all-gather.5.cloned.1.call-start = ((), (), s32[]{:S(2)}) async-start(), calls=%async_computation.1 | async-start | bytes 6684672 | tf_op jit(solution)/shard_map/all_gather | solution.py:56
  13.4 308.3 %all-reduce.3.cloned.1.call-start = ((), (), s32[]{:S(2)}) async-start(), calls=%async_computation.2 | async-start | bytes 18874368 | tf_op jit(solution)/shard_map/psum | solution.py:120
  66.4 6.0 %copy-start.2 = (f32[4,256,4096]{2,1,0:T(8,128)}, f32[4,256,4096]{2,1,0:T(8,128)S(1)}, u32[]{:S(2)}) copy-start(f32[4,256,4096]{2,1,0:T(8,128)S(1)} %get-tuple-element.17) | copy-start | bytes 50331652
  150.5 7.6 %copy-start.4 = (f32[3,1536]{1,0:T(4,128)S(1)}, f32[3,1536]{1,0:T(4,128)}, u32[]{:S(2)}) copy-start(f32[3,1536]{1,0:T(4,128)} %param.17) | copy-start | bytes 55300
  150.5 10.4 %copy-start.5 = (bf16[1,512,1536]{2,1,0:T(8,128)(2,1)S(1)}, bf16[1,512,1536]{2,1,0:T(8,128)(2,1)}, u32[]{:S(2)}) copy-start(bf16[1,512,1536]{2,1,0:T(8,128)(2,1)} %param.19) | copy-start | bytes 4718596
  153.4 4.7 %collective-permute-start = (bf16[1,1536]{1,0:T(2,128)(2,1)S(1)}, bf16[1,1536]{1,0:T(2,128)(2,1)S(1)}, u32[]{:S(2)}, u32[]{:S(2)}) collective-permute-start(bf16[1,1536]{1,0:T(2,128)(2,1)S(1)} %get-tuple-element.12), channel_id=1, source_target_pairs={{0,1},{1,2},{2,3},{3,4},{4,5},{5,6},{6,7},{7,8},{8,9},{9,10},{10,1... | collective-permute-start | bytes 9224 | tf_op jit(solution)/shard_map/ppermute | solution.py:21
  156.6 4.4 collective-permute-start.1
  167.5 269.7 %all-reduce.5.cloned.1.call-start = ((), (), s32[]{:S(2)}) async-start(), calls=%async_computation.3 | async-start | bytes 18874368 | tf_op jit(solution)/shard_map/psum | solution.py:120
  329.3 5.3 %collective-permute-start.2 = (bf16[1,1536]{1,0:T(2,128)(2,1)S(1)}, bf16[1,1536]{1,0:T(2,128)(2,1)S(1)}, u32[]{:S(2)}, u32[]{:S(2)}) collective-permute-start(bf16[1,1536]{1,0:T(2,128)(2,1)S(1)} %get-tuple-element.10), channel_id=1, source_target_pairs={{1,0},{2,1},{3,2},{4,3},{5,4},{6,5},{7,6},{8,7},{9,8},{10,9},{11,1... | collective-permute-start | bytes 9224 | tf_op jit(solution)/shard_map/ppermute | solution.py:23
  330.6 4.8 %collective-permute-start.3 = (bf16[1,1536]{1,0:T(2,128)(2,1)S(1)}, bf16[1,1536]{1,0:T(2,128)(2,1)S(1)}, u32[]{:S(2)}, u32[]{:S(2)}) collective-permute-start(bf16[1,1536]{1,0:T(2,128)(2,1)S(1)} %get-tuple-element.11), channel_id=1, source_target_pairs={{0,1},{1,2},{2,3},{3,4},{4,5},{5,6},{6,7},{7,8},{8,9},{9,10},{10,1... | collective-permute-start | bytes 9224 | tf_op jit(solution)/shard_map/ppermute | solution.py:21
  437.2 7.2 %copy-start.1 = (bf16[768,1536]{1,0:T(8,128)(2,1)S(1)}, bf16[768,1536]{1,0:T(8,128)(2,1)}, u32[]{:S(2)}) copy-start(bf16[768,1536]{1,0:T(8,128)(2,1)} %param.16) | copy-start | bytes 7077892
Sparse Core Ops, SparseCore 0:
  10.7 47.4 all-gather.2
  60.9 61.6 all-gather.4
  167.6 154.0 all-reduce.2
  324.0 113.1 all-reduce.4
